TPU v7x, 32 devices: a whole 2x2x4 slice. The times are simulated.
32 devices in a mesh: seq: 16 (over z, y, core), chan: 2 (over x).
Axes of the slice: x: 2, y: 2, z: 4, core: 2. Of those that a mesh axis runs over, the one named last changes fastest.
Arguments:
- tokens: bfloat16 [2048, 4096], P('seq', 'chan'), may hold values from -6 to 6
- w_in: bfloat16 [4096, 3, 2048], P(None, None, 'chan'), may hold values from -0.09375 to 0.09375
- short_taps: float32 [3, 3, 2048], P(None, None, 'chan'), may hold values from -3 to 3
- skip_gain: float32 [2048], P('chan'), may hold values from 0.5 to 1.5
- filters: float32 [128, 2048], P('chan'), may hold values from -4 to 4
- w_out: bfloat16 [2048, 4096], P('chan'), may hold values from -0.125 to 0.125
Outputs:
- mixed: bfloat16 [2048, 4096], P('seq', 'chan')
All inputs are finite; a program needn't handle non-finite values.
Results may differ from a plain program's by a relative error of at most 0.015.
Values may be sent and summed in bfloat16 or wider, within the bound.
A program may use at most 128 MiB of HBM per device.

v0:
```python
import math

import jax
import jax.numpy as jnp
from jax import lax
from jax.sharding import PartitionSpec as P

GS = 16


def passed_along(block, axis, distance):
    devices = range(lax.axis_size(axis))
    route = [(i - distance, i) for i in devices if i - distance in devices]
    return lax.ppermute(block, axis, route)


def lag_tile(padded_taps, base, size):
    groups = padded_taps.shape[0]
    window = lax.dynamic_slice_in_dim(padded_taps, base + 1, 2 * size - 1, 1)
    turned = window[:, ::-1]
    extra = jnp.concatenate([turned, jnp.zeros((groups, 1), turned.dtype)], axis=1)
    flat = jnp.tile(extra, (1, size))[:, : size * (2 * size - 1)]
    return flat.reshape(groups, size, 2 * size - 1)[:, :, size - 1 :]


def toeplitz_apply(padded_taps, base, block):
    size = block.shape[0]
    tile = lag_tile(padded_taps, base, size)
    return jnp.einsum("gts,sgc->tgc", tile, block, preferred_element_type=jnp.float32)


def shards(tokens, w_in, short_taps, skip_gain, filters, w_out):
    rows = tokens.shape[0]
    width = w_in.shape[0]
    chan_dev = w_in.shape[2]
    flat_in = w_in.reshape(width, 3 * chan_dev)
    proj = jnp.dot(
        lax.all_gather(tokens, "chan", axis=1, tiled=True),
        flat_in,
        preferred_element_type=jnp.float32,
    )
    proj = proj.astype(jnp.bfloat16).reshape(rows, 3, chan_dev)
    earlier = passed_along(proj[rows - 2 :], "seq", 1)
    extended = jnp.concatenate([earlier, proj], axis=0).astype(jnp.float32)
    streams = short_taps[0] * extended[2 : 2 + rows]
    streams = streams + short_taps[1] * extended[1 : 1 + rows]
    streams = streams + short_taps[2] * extended[0:rows]
    gated = (streams[:, 1, :] * streams[:, 2, :]).astype(jnp.bfloat16)
    taps_bf = filters.astype(jnp.bfloat16)
    seq_length = filters.shape[1]
    seq_count = lax.axis_size("seq")
    piece_width = chan_dev // seq_count
    sub_groups = max(piece_width // GS, 1)
    group_width = piece_width // sub_groups
    gathered_z = lax.all_to_all(
        gated.reshape(rows, seq_count, piece_width), "seq", split_axis=1, concat_axis=0, tiled=True
    )
    whole_z = gathered_z.reshape(seq_length, sub_groups, group_width)
    first_group = lax.axis_index("seq") * piece_width // GS
    chosen = lax.dynamic_slice_in_dim(taps_bf, first_group, sub_groups, 0)
    out_block = rows * math.gcd(seq_count, max(1, 512 // rows))
    padded_chosen = jnp.pad(chosen, ((0, 0), (out_block, 0)))

    def one_out(out_step, result):

        def one_in(in_step, running):
            block = lax.dynamic_slice_in_dim(whole_z, in_step * out_block, out_block, 0)
            base = (out_step - in_step) * out_block
            return running + toeplitz_apply(padded_chosen, base, block)

        start_values = jnp.zeros((out_block, sub_groups, group_width), jnp.float32)
        values = lax.fori_loop(0, out_step + 1, one_in, start_values)
        return lax.dynamic_update_slice_in_dim(result, values, out_step * out_block, 0)

    start_result = jnp.zeros((seq_length, sub_groups, group_width), jnp.float32)
    filtered = lax.fori_loop(0, seq_length // out_block, one_out, start_result)
    returned = lax.all_to_all(
        filtered.reshape(seq_length, 1, piece_width), "seq", split_axis=0, concat_axis=1, tiled=True
    )
    long_part = returned.reshape(rows, chan_dev)
    long_out = long_part + skip_gain * gated.astype(jnp.float32)
    mixer = (streams[:, 0, :] * long_out).astype(jnp.bfloat16)
    partial_value = jnp.dot(mixer, w_out, preferred_element_type=jnp.float32)
    return lax.psum_scatter(
        partial_value.astype(jnp.bfloat16), "chan", scatter_dimension=1, tiled=True
    )


def solution(mesh):
    placed = (
        P("seq", "chan"),
        P(None, None, "chan"),
        P(None, None, "chan"),
        P("chan"),
        P("chan", None),
        P("chan", None),
    )
    return jax.shard_map(
        shards, mesh=mesh, in_specs=placed, out_specs=P("seq", "chan"), check_vma=False
    )
```

profile of v0, /device:TPU:0, one launch (start us, length us, event | category | flops | bytes accessed | tf_op | source)
XLA Modules:
  0.0 400.8 jit_solution(11880476445143296836)
XLA Ops:
  7.3 33.4 %copy.33 = bf16[4096,3,1024]{0,2,1:T(8,128)(2,1)} copy(bf16[4096,3,1024]{2,0,1:T(8,128)(2,1)} %param.11) | data formatting | bytes 50331648 | tf_op args[1]
  40.7 13.4 %convolution_convert_fusion.1 = bf16[128,3072]{1,0:T(8,128)(2,1)S(1)} fusion(bf16[128,4096]{1,0:T(8,128)(2,1)} %all-gather.2.cloned.1.call-done, bf16[4096,3072]{0,1:T(8,128)(2,1)} %bitcast.52), kind=kOutput, calls=%fused_computation.10 | convolution fusion | flops 3221618688 | bytes 27000832 | tf_op jit(solution)/shard_map/dot_general | solution.py:37
  62.6 9.2 %all-to-all-start = ((bf16[128,16,64]{0,2,1:T(8,128)(2,1)}), bf16[128,16,64]{0,2,1:T(8,128)(2,1)S(1)}, u32[]{:S(2)}, u32[]{:S(2)}) async-start(bf16[128,16,64]{0,2,1:T(8,128)(2,1)} %bitcast.7), calls=%async_computation | async-start | bytes 524288 | tf_op jit(solution)/shard_map/all_to_all | solution.py:55
  72.1 9.7 %all-to-all-done = bf16[128,16,64]{0,2,1:T(8,128)(2,1)S(1)} async-done(((bf16[128,16,64]{0,2,1:T(8,128)(2,1)}), bf16[128,16,64]{0,2,1:T(8,128)(2,1)S(1)}, u32[]{:S(2)}, u32[]{:S(2)}) %all-to-all-start) | async-done | bytes 262176 | tf_op jit(solution)/shard_map/all_to_all | solution.py:55
  82.2 262.3 %while.47 = (s32[]{:T(128)}, f32[2048,4,16]{0,2,1:T(8,128)S(1)}, bf16[2048,4,16]{0,2,1:T(8,128)(2,1)S(1)}, bf16[4,2560]{1,0:T(4,128)(2,1)S(1)}, s32[]{:T(128)}, ...) while((s32[]{:T(128)}, f32[2048,4,16]{0,2,1:T(8,128)S(1)}, ...), condition=%wide.region_3.4_spmd, body=%wide.region_0.3_spmd.sunk | while | flops 33587212 | bytes 40616448 | solution.py:76
  82.2 26.2 %while.48 = (s32[]{:T(128)}, f32[512,4,16]{0,2,1:T(8,128)S(1)}, s32[]{:T(128)}, bf16[2048,4,16]{0,2,1:T(8,128)(2,1)S(1)}, s32[]{:T(128)}, /*index=5*/bf16[4,2560...) while((s32[]{:T(128)}, f32[512,4,16]{0,2,1:T(8,128)S(1)}, ...), condition=%wide.region_2.2_spmd, body=%wide.region_1.1_spmd.sunk | while | flops 33587212 | bytes 40222928 | solution.py:72
  95.8 10.1 %reshape.51 = bf16[4,512,1023]{2,1,0:T(8,128)(2,1)} reshape(bf16[2095104]{0:T(1024)(128)(2,1)} %reshape.50) | data formatting | bytes 8380416 | tf_op jit(solution)/shard_map/while/body/eval_jaxpr/while/body/reshape | solution.py:23
  108.5 52.4 %while.48 = (s32[]{:T(128)}, f32[512,4,16]{0,2,1:T(8,128)S(1)}, s32[]{:T(128)}, bf16[2048,4,16]{0,2,1:T(8,128)(2,1)S(1)}, s32[]{:T(128)}, /*index=5*/bf16[4,2560...) while((s32[]{:T(128)}, f32[512,4,16]{0,2,1:T(8,128)S(1)}, ...), condition=%wide.region_2.2_spmd, body=%wide.region_1.1_spmd.sunk | while | flops 33587212 | bytes 40222928 | solution.py:72
  122.1 10.1 %reshape.51 = bf16[4,512,1023]{2,1,0:T(8,128)(2,1)} reshape(bf16[2095104]{0:T(1024)(128)(2,1)} %reshape.50) | data formatting | bytes 8380416 | tf_op jit(solution)/shard_map/while/body/eval_jaxpr/while/body/reshape | solution.py:23
  142.6 5.7 %reshape.50 = bf16[2095104]{0:T(1024)(128)(2,1)} reshape(bf16[4,523776]{1,0:T(4,128)(2,1)} %slice.104) | data formatting | bytes 8380416 | tf_op jit(solution)/shard_map/while/body/eval_jaxpr/while
  148.3 10.1 %reshape.51 = bf16[4,512,1023]{2,1,0:T(8,128)(2,1)} reshape(bf16[2095104]{0:T(1024)(128)(2,1)} %reshape.50) | data formatting | bytes 8380416 | tf_op jit(solution)/shard_map/while/body/eval_jaxpr/while/body/reshape | solution.py:23
  161.0 78.6 %while.48 = (s32[]{:T(128)}, f32[512,4,16]{0,2,1:T(8,128)S(1)}, s32[]{:T(128)}, bf16[2048,4,16]{0,2,1:T(8,128)(2,1)S(1)}, s32[]{:T(128)}, /*index=5*/bf16[4,2560...) while((s32[]{:T(128)}, f32[512,4,16]{0,2,1:T(8,128)S(1)}, ...), condition=%wide.region_2.2_spmd, body=%wide.region_1.1_spmd.sunk | while | flops 33587212 | bytes 40222928 | solution.py:72
  168.8 5.7 %reshape.50 = bf16[2095104]{0:T(1024)(128)(2,1)} reshape(bf16[4,523776]{1,0:T(4,128)(2,1)} %slice.104) | data formatting | bytes 8380416 | tf_op jit(solution)/shard_map/while/body/eval_jaxpr/while
  174.6 10.1 %reshape.51 = bf16[4,512,1023]{2,1,0:T(8,128)(2,1)} reshape(bf16[2095104]{0:T(1024)(128)(2,1)} %reshape.50) | data formatting | bytes 8380416 | tf_op jit(solution)/shard_map/while/body/eval_jaxpr/while/body/reshape | solution.py:23
  195.0 5.7 %reshape.50 = bf16[2095104]{0:T(1024)(128)(2,1)} reshape(bf16[4,523776]{1,0:T(4,128)(2,1)} %slice.104) | data formatting | bytes 8380416 | tf_op jit(solution)/shard_map/while/body/eval_jaxpr/while
  200.8 10.1 %reshape.51 = bf16[4,512,1023]{2,1,0:T(8,128)(2,1)} reshape(bf16[2095104]{0:T(1024)(128)(2,1)} %reshape.50) | data formatting | bytes 8380416 | tf_op jit(solution)/shard_map/while/body/eval_jaxpr/while/body/reshape | solution.py:23
  227.0 10.1 %reshape.51 = bf16[4,512,1023]{2,1,0:T(8,128)(2,1)} reshape(bf16[2095104]{0:T(1024)(128)(2,1)} %reshape.50) | data formatting | bytes 8380416 | tf_op jit(solution)/shard_map/while/body/eval_jaxpr/while/body/reshape | solution.py:23
  239.7 104.8 %while.48 = (s32[]{:T(128)}, f32[512,4,16]{0,2,1:T(8,128)S(1)}, s32[]{:T(128)}, bf16[2048,4,16]{0,2,1:T(8,128)(2,1)S(1)}, s32[]{:T(128)}, /*index=5*/bf16[4,2560...) while((s32[]{:T(128)}, f32[512,4,16]{0,2,1:T(8,128)S(1)}, ...), condition=%wide.region_2.2_spmd, body=%wide.region_1.1_spmd.sunk | while | flops 33587212 | bytes 40222928 | solution.py:72
  253.3 10.1 %reshape.51 = bf16[4,512,1023]{2,1,0:T(8,128)(2,1)} reshape(bf16[2095104]{0:T(1024)(128)(2,1)} %reshape.50) | data formatting | bytes 8380416 | tf_op jit(solution)/shard_map/while/body/eval_jaxpr/while/body/reshape | solution.py:23
  279.5 10.1 %reshape.51 = bf16[4,512,1023]{2,1,0:T(8,128)(2,1)} reshape(bf16[2095104]{0:T(1024)(128)(2,1)} %reshape.50) | data formatting | bytes 8380416 | tf_op jit(solution)/shard_map/while/body/eval_jaxpr/while/body/reshape | solution.py:23
  305.7 10.1 %reshape.51 = bf16[4,512,1023]{2,1,0:T(8,128)(2,1)} reshape(bf16[2095104]{0:T(1024)(128)(2,1)} %reshape.50) | data formatting | bytes 8380416 | tf_op jit(solution)/shard_map/while/body/eval_jaxpr/while/body/reshape | solution.py:23
  331.9 10.1 %reshape.51 = bf16[4,512,1023]{2,1,0:T(8,128)(2,1)} reshape(bf16[2095104]{0:T(1024)(128)(2,1)} %reshape.50) | data formatting | bytes 8380416 | tf_op jit(solution)/shard_map/while/body/eval_jaxpr/while/body/reshape | solution.py:23
  346.7 17.4 %all_to_all.30 = f32[16,1,8192]{2,1,0:T(1,128)S(1)} all-to-all(f32[16,1,8192]{2,1,0:T(1,128)S(1)} %reshape.46), channel_id=1, replica_groups=mesh['seq'=16,'chan'=2] {'seq'}, dimensions={0} | all-to-all | bytes 1048576 | tf_op jit(solution)/shard_map/all_to_all | solution.py:77
  374.2 19.8 %reduce-scatter.2.cloned.1.call-done = bf16[128,2048]{1,0:T(8,128)(2,1)} async-done(((bf16[128,4096]{1,0:T(8,128)(2,1)}), bf16[128,2048]{1,0:T(8,128)(2,1)}) %reduce-scatter.2.cloned.1.call-update) | async-done | bytes 524304 | tf_op jit(solution)/shard_map/reduce_scatter | solution.py:84
  (137 shorter events, 165.9 us)
Async XLA Ops:
  6.5 65.5 %copy-start = (f32[64,2048]{1,0:T(8,128)S(1)}, f32[64,2048]{1,0:T(8,128)}, u32[]{:S(2)}) copy-start(f32[64,2048]{1,0:T(8,128)} %param.14) | copy-start | bytes 1572868
  6.5 34.1 %all-gather.2.cloned.1.call-start = ((), (), s32[]{:S(2)}) async-start(), calls=%async_computation.3 | async-start | bytes 1572864 | tf_op jit(solution)/shard_map/all_gather | solution.py:38
  40.7 15.8 %copy-start.4 = (f32[3,3,1024]{2,1,0:T(4,128)S(1)}, f32[3,3,1024]{2,1,0:T(4,128)}, u32[]{:S(2)}) copy-start(f32[3,3,1024]{2,1,0:T(4,128)} %param.12) | copy-start | bytes 110596
  54.1 3.2 collective-permute-start
  60.7 1.2 copy-start.2
  62.6 19.2 %all-to-all-start = ((bf16[128,16,64]{0,2,1:T(8,128)(2,1)}), bf16[128,16,64]{0,2,1:T(8,128)(2,1)S(1)}, u32[]{:S(2)}, u32[]{:S(2)}) async-start(bf16[128,16,64]{0,2,1:T(8,128)(2,1)} %bitcast.7), calls=%async_computation | async-start | bytes 524288 | tf_op jit(solution)/shard_map/all_to_all | solution.py:55
  71.8 322.2 %reduce-scatter.2.cloned.1.call-start = ((), (), s32[]{:S(2)}) async-start(), calls=%async_computation.4 | async-start | bytes 1572864 | tf_op jit(solution)/shard_map/reduce_scatter | solution.py:84
  346.7 21.5 %copy-start.3 = (f32[128,3,1024]{0,2,1:T(8,128)S(1)}, f32[128,3,1024]{0,2,1:T(8,128)}, u32[]{:S(2)}) copy-start(f32[128,3,1024]{0,2,1:T(8,128)} %copy-done.2) | copy-start | bytes 4718596
  346.7 21.5 %copy-start.5 = (f32[1024]{0:T(1024)S(1)}, f32[1024]{0:T(1024)}, u32[]{:S(2)}) copy-start(f32[1024]{0:T(1024)} %param.13) | copy-start | bytes 12292
  368.4 25.5 %copy-start.1 = (f32[64,2048]{1,0:T(8,128)S(1)}, f32[64,2048]{1,0:T(8,128)}, u32[]{:S(2)}) copy-start(f32[64,2048]{1,0:T(8,128)} %param.14) | copy-start | bytes 1572868
Sparse Core Ops, SparseCore 0:
  8.9 23.9 all-gather.1
  374.3 19.6 reduce-scatter.1
where the time goes:
time: 403 us; the launch traced here: 401 us
  local copies, waits for them, and re-layouts  276 us (68%)
  matrix products  44.6 us (11%)
  waiting for transfers between devices  30.7 us (8%)
  blocking collectives  17.4 us (4%)
  between operations  13.7 us (3%)
  starting transfers between devices  11.8 us (3%)
  other arithmetic  6.47 us (2%)
    while x50, local copies, waits for them, and re-layouts  103 us
    reshape x10, local copies, waits for them, and re-layouts, lag_tile(): return flat.reshape(groups, size, 2 * size - 1)[:, :, size - 1:]  101 us
    unnamed x16, local copies, waits for them, and re-layouts  36.9 us
    slice x10, local copies, waits for them, and re-layouts, lag_tile(): flat = jnp.tile(extra, (1, size))[:, :size * (2 * size - 1)]  31.4 us
    dot_general x10, matrix products, toeplitz_apply(): jnp.einsum('gts,sgc->tgc', tile, block, preferred_element_type=jnp.float32)  25.5 us
    reduce_scatter x1, waiting for transfers between devices, shards(): lax.psum_scatter(partial_value.astype(jnp.bfloat16), 'chan', scatter_dime...  19.8 us
    all_to_all x1, blocking collectives, shards(): lax.all_to_all(filtered.reshape(seq_length, 1, piece_width), 'seq', split...  17.4 us
    dot_general x1, matrix products, shards(): jnp.dot(lax.all_gather(tokens, 'chan', axis=1, tiled=True), flat_in, pref...  13.4 us
  transfers between devices with their start and end apart: 4, of which 3 were waited for; matrix products, arithmetic and copies ran while one was open for 8% of the time, Pallas kernels for 0%

commit v1 on v0

v1 whole, which is shorter than its diff:
```python
import functools

import jax
import jax.numpy as jnp
from jax import lax
from jax.experimental import pallas as pl
from jax.experimental.pallas import tpu as pltpu
from jax.sharding import PartitionSpec as P

MESH = pl.DeviceIdType.MESH
BF = jnp.bfloat16
F32 = jnp.float32
LANES = 128
HALO = 8


def dot(a, b):
    return jnp.dot(a, b, preferred_element_type=F32)


def kernel(
    n_seq, n_chan, piece, padded, gs, fc,
    tokens, taps, skip, filters, w_in, w_out,
    out,
    wv, wov, xt, acc, ext, gated, first, toep, zs, zr, ys, lr, hs, hr, ps, pr,
    w_sem, wo_sem, xs_sem, xr_sem, h_sem, z_send, z_recv, y_send, y_recv, p_send, p_recv,
):
    rows, feats = tokens.shape
    width = wv.shape[3]
    parts = feats // fc
    seq, chan = lax.axis_index("seq"), lax.axis_index("chan")

    loads = {}
    for d in range(n_chan):
        source = lax.rem(chan - d + n_chan, n_chan)
        for k in range(parts):
            start = pl.multiple_of(source * feats + k * fc, fc)
            loads[d, k] = pltpu.make_async_copy(
                w_in.at[:, pl.ds(start, fc), :],
                wv.at[d, :, pl.ds(k * fc, fc), :],
                w_sem.at[d, k],
            )
            loads[d, k].start()
    out_loads = {}
    for d in list(range(1, n_chan)) + [0]:
        target = lax.rem(chan + d, n_chan)
        start = pl.multiple_of(target * feats, feats)
        out_loads[d] = pltpu.make_async_copy(
            w_out.at[:, pl.ds(start, feats)], wov.at[d], wo_sem.at[d]
        )
        out_loads[d].start()

    barrier = pltpu.get_barrier_semaphore()
    for d in range(1, n_chan):
        pl.semaphore_signal(
            barrier, inc=1, device_id={"chan": lax.rem(chan + d, n_chan)}, device_id_type=MESH
        )
    for d in range(1, n_seq):
        pl.semaphore_signal(
            barrier, inc=1, device_id={"seq": lax.rem(seq + d, n_seq)}, device_id_type=MESH
        )
    pl.semaphore_wait(barrier, n_chan - 1 + n_seq - 1)

    token_sends = {}
    for k in range(parts):
        for d in range(1, n_chan):
            token_sends[d, k] = pltpu.make_async_remote_copy(
                src_ref=tokens.at[:, pl.ds(k * fc, fc)],
                dst_ref=xt.at[d - 1, :, pl.ds(k * fc, fc)],
                send_sem=xs_sem.at[d - 1, k],
                recv_sem=xr_sem.at[d - 1, k],
                device_id={"chan": lax.rem(chan + d, n_chan)},
                device_id_type=MESH,
            )
            token_sends[d, k].start()

    def project(d, k):
        loads[d, k].wait()
        part = pl.ds(k * fc, fc)
        x = tokens[:, part] if d == 0 else xt[d - 1, :, part]
        for j in range(3):
            term = dot(x, wv[d, j, part, :])
            if d == 0 and k == 0:
                acc[j] = term
            else:
                acc[j] += term

    for k in range(parts):
        project(0, k)

    length = toep.shape[2]
    groups = toep.shape[0]
    first_group = seq * piece // gs
    later = lax.broadcasted_iota(jnp.int32, (rows, rows), 1) >= lax.broadcasted_iota(
        jnp.int32, (rows, rows), 0
    )
    for g in range(groups):
        row = filters[pl.ds(first_group + g, 1), :].astype(BF).astype(F32)
        spread = jnp.broadcast_to(row, (rows, length))
        turned = pltpu.roll(spread, 0, 1, stride=1, stride_axis=0)
        toep[g, :, rows:] = turned[:, rows:].astype(BF)
        toep[g, :, :rows] = jnp.where(later, turned[:, :rows], 0.0).astype(BF)

    for k in range(parts):
        for d in range(1, n_chan):
            token_sends[d, k].wait_recv()
            project(d, k)

    for j in range(3):
        ext[j, HALO:, :] = acc[j].astype(BF).astype(F32)
        hs[2 * j : 2 * j + 2, :] = ext[j, HALO + rows - 2 :, :]
    halo = pltpu.make_async_remote_copy(
        src_ref=hs,
        dst_ref=hr,
        send_sem=h_sem.at[0],
        recv_sem=h_sem.at[1],
        device_id={"seq": lax.rem(seq + 1, n_seq)},
        device_id_type=MESH,
    )
    halo.start()
    halo.wait()
    has_past = seq > 0
    for j in range(3):
        ext[j, HALO - 2 : HALO, :] = jnp.where(has_past, hr[2 * j : 2 * j + 2, :], 0.0)

    def stream(j, cols):
        value = taps[j : j + 1, cols] * ext[j, HALO:, cols]
        value = value + taps[3 + j : 4 + j, cols] * ext[j, HALO - 1 : HALO - 1 + rows, cols]
        return value + taps[6 + j : 7 + j, cols] * ext[j, HALO - 2 : HALO - 2 + rows, cols]

    per = LANES // piece
    for b in range(width // LANES):
        cols = pl.ds(b * LANES, LANES)
        z = (stream(1, cols) * stream(2, cols)).astype(BF).astype(F32)
        gated[:, cols] = z
        turned = z.T.reshape(per, piece, rows)
        if padded > piece:
            fill = jnp.zeros((per, padded - piece, rows), F32)
            turned = jnp.concatenate([turned, fill], axis=1)
        zs[b * per : (b + 1) * per] = turned.astype(BF)

    def exchange(source, target, send, recv):
        copies = []
        for d in range(1, n_seq):
            other = lax.rem(seq + d, n_seq)
            copies.append(
                pltpu.make_async_remote_copy(
                    src_ref=source.at[other],
                    dst_ref=target.at[seq],
                    send_sem=send.at[d - 1],
                    recv_sem=recv.at[d - 1],
                    device_id={"seq": other},
                    device_id_type=MESH,
                )
            )
            copies[-1].start()
        target[seq] = source[seq]
        return copies

    z_copies = exchange(zs, zr, z_send, z_recv)
    for b in range(width // LANES):
        cols = pl.ds(b * LANES, LANES)
        first[:, cols] = stream(0, cols)
    for copy in z_copies:
        copy.wait()

    wide = padded // groups
    lags = 2 if n_seq % 2 == 0 else 1
    for g in range(groups):
        x = zr[:, g * wide : (g + 1) * wide, :].reshape(n_seq * wide, rows)
        total = None
        for e in range(0, n_seq, lags):
            rest = (n_seq - e) * wide
            both = dot(x[:rest], toep[g, :, e * rows : (e + lags) * rows])
            for i in range(lags):
                held = (n_seq - e - i) * wide
                term = both[:held, i * rows : (i + 1) * rows]
                if e + i:
                    term = jnp.concatenate(
                        [jnp.zeros(((e + i) * wide, rows), F32), term], axis=0
                    )
                total = term if total is None else total + term
        ys[:, g * wide : (g + 1) * wide, :] = total.astype(BF).reshape(n_seq, wide, rows)

    for copy in exchange(ys, lr, y_send, y_recv):
        copy.wait()

    mixers = []
    for b in range(width // LANES):
        cols = pl.ds(b * LANES, LANES)
        turned = lr[b * per : (b + 1) * per].astype(F32)[:, :piece, :]
        filtered = turned.reshape(LANES, rows).T
        long_out = filtered + skip[:, cols] * gated[:, cols]
        mixers.append((first[:, cols] * long_out).astype(BF))
    mixer = jnp.concatenate(mixers, axis=1)

    part_sends = []
    for d in range(1, n_chan):
        out_loads[d].wait()
        for k in range(parts):
            part = pl.ds(k * fc, fc)
            ps[d - 1, :, part] = dot(mixer, wov[d, :, part]).astype(BF)
            copy = pltpu.make_async_remote_copy(
                src_ref=ps.at[d - 1, :, part],
                dst_ref=pr.at[d - 1, :, part],
                send_sem=p_send.at[d - 1, k],
                recv_sem=p_recv.at[d - 1, k],
                device_id={"chan": lax.rem(chan + d, n_chan)},
                device_id_type=MESH,
            )
            copy.start()
            part_sends.append((d, k, copy))
    out_loads[0].wait()
    sums = []
    for k in range(parts):
        part = pl.ds(k * fc, fc)
        sums.append(dot(mixer, wov[0, :, part]).astype(BF).astype(F32))
    for d, k, copy in part_sends:
        copy.wait_recv()
        part = pl.ds(k * fc, fc)
        sums[k] = sums[k] + pr[d - 1, :, part].astype(F32)
        if d == n_chan - 1:
            out[:, part] = sums[k].astype(BF)
    for d, k, copy in part_sends:
        copy.wait_send()
    for copy in token_sends.values():
        copy.wait_send()


def shards(n_seq, n_chan, tokens, w_in, short_taps, skip_gain, filters, w_out):
    rows, feats = tokens.shape
    width = w_in.shape[2]
    length = filters.shape[1]
    piece = width // n_seq
    gs = width // filters.shape[0]
    padded = max(piece, 16)
    groups = max(piece // gs, 1)
    fc = min(feats, 512)
    parts = feats // fc
    others = max(n_chan - 1, 1)
    vmem = pl.BlockSpec(memory_space=pltpu.VMEM)
    hbm = pl.BlockSpec(memory_space=pl.ANY)
    sem = pltpu.SemaphoreType.DMA
    return pl.pallas_call(
        functools.partial(kernel, n_seq, n_chan, piece, padded, gs, fc),
        out_shape=jax.ShapeDtypeStruct((rows, feats), BF),
        in_specs=[vmem, vmem, vmem, vmem, hbm, hbm],
        out_specs=vmem,
        scratch_shapes=[
            pltpu.VMEM((n_chan, 3, feats, width), BF),
            pltpu.VMEM((n_chan, width, feats), BF),
            pltpu.VMEM((others, rows, feats), BF),
            pltpu.VMEM((3, rows, width), F32),
            pltpu.VMEM((3, HALO + rows, width), F32),
            pltpu.VMEM((rows, width), F32),
            pltpu.VMEM((rows, width), F32),
            pltpu.VMEM((groups, rows, length), BF),
            pltpu.VMEM((n_seq, padded, rows), BF),
            pltpu.VMEM((n_seq, padded, rows), BF),
            pltpu.VMEM((n_seq, padded, rows), BF),
            pltpu.VMEM((n_seq, padded, rows), BF),
            pltpu.VMEM((HALO, width), F32),
            pltpu.VMEM((HALO, width), F32),
            pltpu.VMEM((others, rows, feats), BF),
            pltpu.VMEM((others, rows, feats), BF),
            sem((n_chan, parts)),
            sem((n_chan,)),
            sem((others, parts)),
            sem((others, parts)),
            sem((2,)),
            sem((n_seq,)),
            sem((n_seq,)),
            sem((n_seq,)),
            sem((n_seq,)),
            sem((others, parts)),
            sem((others, parts)),
        ],
        compiler_params=pltpu.CompilerParams(
            collective_id=0, has_side_effects=True, vmem_limit_bytes=58 * 1024 * 1024
        ),
    )(
        tokens,
        short_taps.reshape(9, width),
        skip_gain.reshape(1, width),
        filters,
        jnp.transpose(w_in, (1, 0, 2)),
        w_out,
    )


def solution(mesh):
    placed = (
        P("seq", "chan"),
        P(None, None, "chan"),
        P(None, None, "chan"),
        P("chan"),
        P("chan", None),
        P("chan", None),
    )
    return jax.shard_map(
        functools.partial(shards, mesh.shape["seq"], mesh.shape["chan"]),
        mesh=mesh,
        in_specs=placed,
        out_specs=P("seq", "chan"),
        check_vma=False,
    )
```

time: 403 us -> 55 us (0.14)
  local copies, waits for them, and re-layouts: 276 us -> 3.33 us
  Pallas kernels: 0 us -> 51.5 us
  matrix products: 44.6 us -> 0 us
  waiting for transfers between devices: 30.7 us -> 0 us
  blocking collectives: 17.4 us -> 0 us
  between operations: 13.7 us -> 0.01 us
  starting transfers between devices: 11.8 us -> 0 us
  other arithmetic: 6.47 us -> 0 us
    while x50 -> x0, local copies, waits for them, and re-layouts: 103 us -> none
    reshape x12 -> x1, local copies, waits for them, and re-layouts: 101 us -> 1.45 us  [shards(): short_taps.reshape(9, width)]
    pallas_call x0 -> x1, Pallas kernels: none -> 51.5 us  [shards(): pl.pallas_call(functools.partial(kernel, n_seq, n_chan, piece, padded, gs...]
    dot_general x12 -> x0, matrix products: 44.6 us -> none  [the longest x10 25.5 us: toeplitz_apply(): jnp.einsum('gts,sgc->tgc', tile, block, preferred_element_type=jnp.float32)]
    unnamed x16 -> x1, local copies, waits for them, and re-layouts: 36.9 us -> 1.88 us
    slice x12 -> x0, local copies, waits for them, and re-layouts: 31.4 us -> none  [the longest x10 31.4 us: lag_tile(): flat = jnp.tile(extra, (1, size))[:, :size * (2 * size - 1)]]
    reduce_scatter x1 -> x0, waiting for transfers between devices: 19.8 us -> none  [shards(): lax.psum_scatter(partial_value.astype(jnp.bfloat16), 'chan', scatter_dime...]
    all_to_all x1 -> x0, blocking collectives: 17.4 us -> none  [shards(): lax.all_to_all(filtered.reshape(seq_length, 1, piece_width), 'seq', split...]
  transfers between devices with their start and end apart: 4 -> 0, of which waited for: 3 -> 0; matrix products, arithmetic and copies ran while one was open for 8% -> 0% of each run, Pallas kernels for 0% -> 0%
where the time goes in v1:
time: 55 us; the launch traced here: 54.8 us
  Pallas kernels  51.5 us (94%)
  local copies, waits for them, and re-layouts  3.33 us (6%)
    pallas_call x1, Pallas kernels, shards(): pl.pallas_call(functools.partial(kernel, n_seq, n_chan, piece, padded, gs...  51.5 us
    unnamed x1, local copies, waits for them, and re-layouts  1.88 us
    reshape x1, local copies, waits for them, and re-layouts, shards(): short_taps.reshape(9, width)  1.45 us

profile of v1, /device:TPU:0, one launch (start us, length us, event | category | flops | bytes accessed | tf_op | source)
XLA Modules:
  0.0 54.8 jit_solution(9857163730834329465)
XLA Ops:
  0.0 1.4 %reshape.6.taps = f32[9,1024]{1,0:T(8,128)} reshape(f32[3,3,1024]{2,1,0:T(4,128)} %param.8) | data formatting | bytes 73728 | tf_op jit(solution)/shard_map/reshape | solution.py:283
  1.4 51.5 %shard_map.64 = bf16[128,2048]{1,0:T(8,128)(2,1)} custom-call(bf16[128,2048]{1,0:T(8,128)(2,1)} %tokens.1, f32[9,1024]{1,0:T(8,128)} %reshape.6.taps, f32[1,1024]{1,0:T(1,128)} %bitcast.3, f32[64,2048]{1,0:T(8,128)} %filters.1, bf16[3,4096,1024]{2,1,0:T(8,128)(2,1)} %bitcast.2, bf16[1024,4096]{1,0:T(8,128)(2,1)} %w_out.1), custom_call_target="tpu_custom_call" | custom-call | tf_op jit(solution)/shard_map/pallas_call | solution.py:244
  52.9 1.9 %copy.8 = bf16[128,2048]{1,0:T(8,128)(2,1)} copy(bf16[128,2048]{1,0:T(8,128)(2,1)} %shard_map.64) | data formatting | bytes 1048576

commit v2 on v1

v2 whole, which is shorter than its diff:
```python
import functools

import jax
import jax.numpy as jnp
from jax import lax
from jax.experimental import pallas as pl
from jax.experimental.pallas import tpu as pltpu
from jax.sharding import PartitionSpec as P

MESH = pl.DeviceIdType.MESH
BF = jnp.bfloat16
F32 = jnp.float32
LANES = 128
HALO = 8


def dot(a, b):
    return jnp.dot(a, b, preferred_element_type=F32)


def kernel(
    n_seq, n_chan, halves, piece, padded, gs, fc, fo,
    tokens, taps, skip, filters, w_in, w_out,
    out,
    tv, fv, wv, wov, xt, acc, ext, gated, first, toep, zs, zr, ys, lr, hs, hr, ps, pr,
    w_sem, wo_sem, l_sem, xs_sem, xr_sem, h_send, h_recv,
    z_send, z_recv, y_send, y_recv, p_send, p_recv,
):
    rows, feats = tv.shape
    width = wv.shape[3]
    half = width // halves
    parts = feats // fc
    seq, chan = lax.axis_index("seq"), lax.axis_index("chan")

    def load(d, k):
        source = lax.rem(chan - d + n_chan, n_chan)
        start = pl.multiple_of(source * feats + k * fc, fc)
        return pltpu.make_async_copy(
            w_in.at[:, pl.ds(start, fc), :],
            wv.at[d, :, pl.ds(k * fc, fc), :],
            w_sem.at[d, k],
        )

    def out_load(d):
        target = lax.rem(chan + d, n_chan)
        start = pl.multiple_of(target * feats, feats)
        return pltpu.make_async_copy(
            w_out.at[:, pl.ds(start, feats)], wov.at[d], wo_sem.at[d]
        )

    barrier = pltpu.get_barrier_semaphore()
    for d in range(1, n_chan):
        pl.semaphore_signal(
            barrier, inc=1, device_id={"chan": lax.rem(chan + d, n_chan)}, device_id_type=MESH
        )
    for d in range(1, n_seq):
        pl.semaphore_signal(
            barrier, inc=1, device_id={"seq": lax.rem(seq + d, n_seq)}, device_id_type=MESH
        )
    token_load = pltpu.make_async_copy(tokens, tv, l_sem.at[0])
    token_load.start()
    early = min(2, parts)
    for k in range(early):
        load(0, k).start()
    token_load.wait()
    pl.semaphore_wait(barrier, n_chan - 1 + n_seq - 1)

    token_sends = {}
    for k in range(parts):
        for d in range(1, n_chan):
            token_sends[d, k] = pltpu.make_async_remote_copy(
                src_ref=tv.at[:, pl.ds(k * fc, fc)],
                dst_ref=xt.at[d - 1, :, pl.ds(k * fc, fc)],
                send_sem=xs_sem.at[d - 1, k],
                recv_sem=xr_sem.at[d - 1, k],
                device_id={"chan": lax.rem(chan + d, n_chan)},
                device_id_type=MESH,
            )
            token_sends[d, k].start()
    for k in range(early, parts):
        load(0, k).start()
    filter_load = pltpu.make_async_copy(filters, fv, l_sem.at[1])
    filter_load.start()

    def project(d, k, cols):
        part = pl.ds(k * fc, fc)
        x = tv[:, part] if d == 0 else xt[d - 1, :, part]
        for j in range(3):
            term = dot(x, wv[d, j, part, cols])
            if d == 0 and k == 0:
                acc[j, :, cols] = term
            else:
                acc[j, :, cols] += term

    every = pl.ds(0, width)
    for k in range(parts):
        load(0, k).wait()
        for d in range(1, n_chan):
            load(d, k).start()
        project(0, k, every)

    length = toep.shape[3]
    groups = toep.shape[1]
    later = lax.broadcasted_iota(jnp.int32, (rows, rows), 1) >= lax.broadcasted_iota(
        jnp.int32, (rows, rows), 0
    )
    filter_load.wait()
    for h in range(halves):
        first_group = h * (half // gs) + seq * piece // gs
        for g in range(groups):
            row = fv[pl.ds(first_group + g, 1), :].astype(BF).astype(F32)
            spread = jnp.broadcast_to(row, (rows, length))
            turned = pltpu.roll(spread, 0, 1, stride=1, stride_axis=0)
            toep[h, g, :, rows:] = turned[:, rows:].astype(BF)
            toep[h, g, :, :rows] = jnp.where(later, turned[:, :rows], 0.0).astype(BF)

    sections = [pl.ds(h * half, half) for h in range(halves)]
    halos = []
    for k in range(parts):
        for d in range(1, n_chan):
            load(d, k).wait()
            token_sends[d, k].wait_recv()
            if k < parts - 1 or d < n_chan - 1:
                project(d, k, every)
    for h, cols in enumerate(sections):
        project(n_chan - 1, parts - 1, cols)
        for j in range(3):
            ext[j, HALO:, cols] = acc[j, :, cols].astype(BF).astype(F32)
            hs[h, 2 * j : 2 * j + 2, :] = ext[j, HALO + rows - 2 :, cols]
        halos.append(
            pltpu.make_async_remote_copy(
                src_ref=hs.at[h],
                dst_ref=hr.at[h],
                send_sem=h_send.at[h],
                recv_sem=h_recv.at[h],
                device_id={"seq": lax.rem(seq + 1, n_seq)},
                device_id_type=MESH,
            )
        )
        halos[-1].start()

    for d in list(range(1, n_chan)) + [0]:
        out_load(d).start()

    def stream(j, cols):
        value = taps[0, j : j + 1, cols] * ext[j, HALO:, cols]
        value = value + taps[1, j : j + 1, cols] * ext[j, HALO - 1 : HALO - 1 + rows, cols]
        return value + taps[2, j : j + 1, cols] * ext[j, HALO - 2 : HALO - 2 + rows, cols]

    def exchange(source, target, send, recv):
        copies = []
        for d in range(1, n_seq):
            other = lax.rem(seq + d, n_seq)
            copies.append(
                pltpu.make_async_remote_copy(
                    src_ref=source.at[other],
                    dst_ref=target.at[seq],
                    send_sem=send.at[d - 1],
                    recv_sem=recv.at[d - 1],
                    device_id={"seq": other},
                    device_id_type=MESH,
                )
            )
            copies[-1].start()
        target[seq] = source[seq]
        return copies

    has_past = seq > 0
    per = LANES // piece
    tiles = half // LANES
    z_copies, y_copies = [], []
    for h, cols in enumerate(sections):
        halos[h].wait()
        for j in range(3):
            ext[j, HALO - 2 : HALO, cols] = jnp.where(has_past, hr[h, 2 * j : 2 * j + 2, :], 0.0)
        for b in range(tiles):
            cols = pl.ds(h * half + b * LANES, LANES)
            z = (stream(1, cols) * stream(2, cols)).astype(BF).astype(F32)
            gated[:, cols] = z
            turned = z.T.reshape(per, piece, rows)
            if padded > piece:
                fill = jnp.zeros((per, padded - piece, rows), F32)
                turned = jnp.concatenate([turned, fill], axis=1)
            zs[h, b * per : (b + 1) * per] = turned.astype(BF)
        z_copies.append(exchange(zs.at[h], zr.at[h], z_send.at[h], z_recv.at[h]))
    for b in range(width // LANES):
        cols = pl.ds(b * LANES, LANES)
        first[:, cols] = stream(0, cols)

    wide = padded // groups
    lags = 2 if n_seq % 2 == 0 else 1
    for h in range(halves):
        for copy in z_copies[h]:
            copy.wait_recv()
        for g in range(groups):
            x = zr[h, :, g * wide : (g + 1) * wide, :].reshape(n_seq * wide, rows)
            total = None
            for e in range(0, n_seq, lags):
                rest = (n_seq - e) * wide
                both = dot(x[:rest], toep[h, g, :, e * rows : (e + lags) * rows])
                for i in range(lags):
                    held = (n_seq - e - i) * wide
                    term = both[:held, i * rows : (i + 1) * rows]
                    if e + i:
                        term = jnp.concatenate(
                            [jnp.zeros(((e + i) * wide, rows), F32), term], axis=0
                        )
                    total = term if total is None else total + term
            ys[h, :, g * wide : (g + 1) * wide, :] = total.astype(BF).reshape(n_seq, wide, rows)
        y_copies.append(exchange(ys.at[h], lr.at[h], y_send.at[h], y_recv.at[h]))

    mixers = []
    for h in range(halves):
        for copy in y_copies[h]:
            copy.wait_recv()
        for b in range(tiles):
            cols = pl.ds(h * half + b * LANES, LANES)
            turned = lr[h, b * per : (b + 1) * per].astype(F32)[:, :piece, :]
            filtered = turned.reshape(LANES, rows).T
            long_out = filtered + skip[:, cols] * gated[:, cols]
            mixers.append((first[:, cols] * long_out).astype(BF))
    mixer = jnp.concatenate(mixers, axis=1)

    part_sends = []
    for d in range(1, n_chan):
        out_load(d).wait()
        for k in range(feats // fo):
            part = pl.ds(k * fo, fo)
            ps[d - 1, :, part] = dot(mixer, wov[d, :, part]).astype(BF)
            copy = pltpu.make_async_remote_copy(
                src_ref=ps.at[d - 1, :, part],
                dst_ref=pr.at[d - 1, :, part],
                send_sem=p_send.at[d - 1, k],
                recv_sem=p_recv.at[d - 1, k],
                device_id={"chan": lax.rem(chan + d, n_chan)},
                device_id_type=MESH,
            )
            copy.start()
            part_sends.append((d, k, copy))
    out_load(0).wait()
    sums = []
    for k in range(feats // fo):
        part = pl.ds(k * fo, fo)
        sums.append(dot(mixer, wov[0, :, part]).astype(BF).astype(F32))
    for copies in z_copies + y_copies:
        for copy in copies:
            copy.wait_send()
    for copy in token_sends.values():
        copy.wait_send()
    for d, k, copy in part_sends:
        copy.wait_recv()
        part = pl.ds(k * fo, fo)
        sums[k] = sums[k] + pr[d - 1, :, part].astype(F32)
        if d == n_chan - 1:
            out[:, part] = sums[k].astype(BF)
    for d, k, copy in part_sends:
        copy.wait_send()


def shards(n_seq, n_chan, tokens, w_in, short_taps, skip_gain, filters, w_out):
    rows, feats = tokens.shape
    width = w_in.shape[2]
    length = filters.shape[1]
    gs = width // filters.shape[0]
    halves = 2 if width % (2 * n_seq * gs) == 0 else 1
    half = width // halves
    piece = half // n_seq
    padded = max(piece, 16)
    groups = max(piece // gs, 1)
    fc = min(feats, 512)
    fo = min(feats, 256)
    parts, cuts = feats // fc, feats // fo
    others = max(n_chan - 1, 1)
    vmem = pl.BlockSpec(memory_space=pltpu.VMEM)
    hbm = pl.BlockSpec(memory_space=pl.ANY)
    sem = pltpu.SemaphoreType.DMA
    return pl.pallas_call(
        functools.partial(kernel, n_seq, n_chan, halves, piece, padded, gs, fc, fo),
        out_shape=jax.ShapeDtypeStruct((rows, feats), BF),
        in_specs=[hbm, vmem, vmem, hbm, hbm, hbm],
        out_specs=vmem,
        scratch_shapes=[
            pltpu.VMEM((rows, feats), BF),
            pltpu.VMEM(filters.shape, F32),
            pltpu.VMEM((n_chan, 3, feats, width), BF),
            pltpu.VMEM((n_chan, width, feats), BF),
            pltpu.VMEM((others, rows, feats), BF),
            pltpu.VMEM((3, rows, width), F32),
            pltpu.VMEM((3, HALO + rows, width), F32),
            pltpu.VMEM((rows, width), F32),
            pltpu.VMEM((rows, width), F32),
            pltpu.VMEM((halves, groups, rows, length), BF),
            pltpu.VMEM((halves, n_seq, padded, rows), BF),
            pltpu.VMEM((halves, n_seq, padded, rows), BF),
            pltpu.VMEM((halves, n_seq, padded, rows), BF),
            pltpu.VMEM((halves, n_seq, padded, rows), BF),
            pltpu.VMEM((halves, HALO, half), F32),
            pltpu.VMEM((halves, HALO, half), F32),
            pltpu.VMEM((others, rows, feats), BF),
            pltpu.VMEM((others, rows, feats), BF),
            sem((n_chan, parts)),
            sem((n_chan,)),
            sem((2,)),
            sem((others, parts)),
            sem((others, parts)),
            sem((halves,)),
            sem((halves,)),
            sem((halves, n_seq)),
            sem((halves, n_seq)),
            sem((halves, n_seq)),
            sem((halves, n_seq)),
            sem((others, cuts)),
            sem((others, cuts)),
        ],
        compiler_params=pltpu.CompilerParams(
            collective_id=0, has_side_effects=True, vmem_limit_bytes=58 * 1024 * 1024
        ),
    )(
        tokens,
        short_taps,
        skip_gain.reshape(1, width),
        filters,
        jnp.transpose(w_in, (1, 0, 2)),
        w_out,
    )


def solution(mesh):
    placed = (
        P("seq", "chan"),
        P(None, None, "chan"),
        P(None, None, "chan"),
        P("chan"),
        P("chan", None),
        P("chan", None),
    )
    return jax.shard_map(
        functools.partial(shards, mesh.shape["seq"], mesh.shape["chan"]),
        mesh=mesh,
        in_specs=placed,
        out_specs=P("seq", "chan"),
        check_vma=False,
    )
```

time: 55 us -> 53 us (0.964)
  local copies, waits for them, and re-layouts: 3.33 us -> 1.88 us
  Pallas kernels: 51.5 us -> 50.9 us
    reshape x1 -> x0, local copies, waits for them, and re-layouts: 1.45 us -> none  [shards(): short_taps.reshape(9, width)]
    pallas_call x1, Pallas kernels: 51.5 us -> 50.9 us  [shards(): pl.pallas_call(functools.partial(kernel, n_seq, n_chan, halves, piece, pa...]
where the time goes in v2:
time: 53 us; the launch traced here: 52.8 us
  Pallas kernels  50.9 us (96%)
  local copies, waits for them, and re-layouts  1.88 us (4%)
    pallas_call x1, Pallas kernels, shards(): pl.pallas_call(functools.partial(kernel, n_seq, n_chan, halves, piece, pa...  50.9 us
    unnamed x1, local copies, waits for them, and re-layouts  1.88 us

profile of v2, /device:TPU:0, one launch (start us, length us, event | category | flops | bytes accessed | tf_op | source)
XLA Modules:
  0.0 52.8 jit_solution(11325464433705282438)
XLA Ops:
  0.0 50.9 %shard_map.64 = bf16[128,2048]{1,0:T(8,128)(2,1)} custom-call(bf16[128,2048]{1,0:T(8,128)(2,1)} %tokens.1, f32[3,3,1024]{2,1,0:T(4,128)} %taps.1, f32[1,1024]{1,0:T(1,128)} %bitcast.3, f32[64,2048]{1,0:T(8,128)} %filters.1, bf16[3,4096,1024]{2,1,0:T(8,128)(2,1)} %bitcast.2, bf16[1024,4096]{1,0:T(8,128)(2,1)} %w_out.1), custom_call_target="tpu_custom_call" | custom-call | tf_op jit(solution)/shard_map/pallas_call | solution.py:277
  50.9 1.9 %copy.8 = bf16[128,2048]{1,0:T(8,128)(2,1)} copy(bf16[128,2048]{1,0:T(8,128)(2,1)} %shard_map.64) | data formatting | bytes 1048576

commit v3 on v2

--- a/solution.py
+++ b/solution.py
@@ -24,7 +24,7 @@
     out,
     tv, fv, wv, wov, xt, acc, ext, gated, first, toep, zs, zr, ys, lr, hs, hr, ps, pr,
     w_sem, wo_sem, l_sem, xs_sem, xr_sem, h_send, h_recv,
-    z_send, z_recv, y_send, y_recv, p_send, p_recv,
+    z_send, z_recv, y_send, y_recv, p_send, p_recv, rounds,
 ):
     rows, feats = tv.shape
     width = wv.shape[3]
@@ -53,17 +53,20 @@
         pl.semaphore_signal(
             barrier, inc=1, device_id={"chan": lax.rem(chan + d, n_chan)}, device_id_type=MESH
         )
-    for d in range(1, n_seq):
-        pl.semaphore_signal(
-            barrier, inc=1, device_id={"seq": lax.rem(seq + d, n_seq)}, device_id_type=MESH
-        )
+    pairs = []
+    bit = 1
+    while bit < n_seq:
+        pairs.append(seq + bit * (1 - 2 * lax.rem(lax.div(seq, bit), 2)))
+        bit *= 2
+    for other in pairs:
+        pl.semaphore_signal(barrier, inc=1, device_id={"seq": other}, device_id_type=MESH)
     token_load = pltpu.make_async_copy(tokens, tv, l_sem.at[0])
     token_load.start()
     early = min(2, parts)
     for k in range(early):
         load(0, k).start()
     token_load.wait()
-    pl.semaphore_wait(barrier, n_chan - 1 + n_seq - 1)
+    pl.semaphore_wait(barrier, n_chan - 1 + len(pairs))
 
     token_sends = {}
     for k in range(parts):
@@ -92,12 +95,27 @@
             else:
                 acc[j, :, cols] += term
 
+    def round_signal(i):
+        if i < len(pairs):
+            pl.semaphore_signal(
+                rounds.at[i], inc=1, device_id={"seq": pairs[i]}, device_id_type=MESH
+            )
+
+    def round_end(i):
+        if i < len(pairs):
+            pl.semaphore_wait(rounds.at[i], 1)
+            round_signal(i + 1)
+
     every = pl.ds(0, width)
+    round_signal(0)
     for k in range(parts):
         load(0, k).wait()
         for d in range(1, n_chan):
             load(d, k).start()
         project(0, k, every)
+        round_end(k)
+    for k in range(parts, len(pairs)):
+        round_end(k)
 
     length = toep.shape[3]
     groups = toep.shape[1]
@@ -311,6 +329,7 @@
             sem((halves, n_seq)),
             sem((others, cuts)),
             sem((others, cuts)),
+            pltpu.SemaphoreType.REGULAR((n_seq.bit_length(),)),
         ],
         compiler_params=pltpu.CompilerParams(
             collective_id=0, has_side_effects=True, vmem_limit_bytes=58 * 1024 * 1024

time: 53 us -> 52.8 us (level)
  no operation moved by 1% of the time
where the time goes in v3:
time: 52.8 us; the launch traced here: 52.6 us
  Pallas kernels  50.7 us (96%)
  local copies, waits for them, and re-layouts  1.88 us (4%)
    pallas_call x1, Pallas kernels, shards(): pl.pallas_call(functools.partial(kernel, n_seq, n_chan, halves, piece, pa...  50.7 us
    unnamed x1, local copies, waits for them, and re-layouts  1.88 us

profile of v3, /device:TPU:0, one launch (start us, length us, event | category | flops | bytes accessed | tf_op | source)
XLA Modules:
  0.0 52.6 jit_solution(7122468529751458994)
XLA Ops:
  0.0 50.7 %shard_map.64 = bf16[128,2048]{1,0:T(8,128)(2,1)} custom-call(bf16[128,2048]{1,0:T(8,128)(2,1)} %tokens.1, f32[3,3,1024]{2,1,0:T(4,128)} %taps.1, f32[1,1024]{1,0:T(1,128)} %bitcast.3, f32[64,2048]{1,0:T(8,128)} %filters.1, bf16[3,4096,1024]{2,1,0:T(8,128)(2,1)} %bitcast.2, bf16[1024,4096]{1,0:T(8,128)(2,1)} %w_out.1), custom_call_target="tpu_custom_call" | custom-call | tf_op jit(solution)/shard_map/pallas_call | solution.py:295
  50.7 1.9 %copy.8 = bf16[128,2048]{1,0:T(8,128)(2,1)} copy(bf16[128,2048]{1,0:T(8,128)(2,1)} %shard_map.64) | data formatting | bytes 1048576

commit v4 on v3

--- a/solution.py
+++ b/solution.py
@@ -62,9 +62,6 @@
         pl.semaphore_signal(barrier, inc=1, device_id={"seq": other}, device_id_type=MESH)
     token_load = pltpu.make_async_copy(tokens, tv, l_sem.at[0])
     token_load.start()
-    early = min(2, parts)
-    for k in range(early):
-        load(0, k).start()
     token_load.wait()
     pl.semaphore_wait(barrier, n_chan - 1 + len(pairs))
 
@@ -80,7 +77,7 @@
                 device_id_type=MESH,
             )
             token_sends[d, k].start()
-    for k in range(early, parts):
+    for k in range(parts):
         load(0, k).start()
     filter_load = pltpu.make_async_copy(filters, fv, l_sem.at[1])
     filter_load.start()
@@ -167,7 +164,7 @@
 
     def exchange(source, target, send, recv):
         copies = []
-        for d in range(1, n_seq):
+        for d in sorted(range(1, n_seq), key=lambda d: -min(d, n_seq - d)):
             other = lax.rem(seq + d, n_seq)
             copies.append(
                 pltpu.make_async_remote_copy(
@@ -285,7 +282,7 @@
     piece = half // n_seq
     padded = max(piece, 16)
     groups = max(piece // gs, 1)
-    fc = min(feats, 512)
+    fc = min(feats, 256)
     fo = min(feats, 256)
     parts, cuts = feats // fc, feats // fo
     others = max(n_chan - 1, 1)

time: 52.8 us -> 52.2 us (0.989)
  Pallas kernels: 50.7 us -> 50.1 us
    pallas_call x1, Pallas kernels: 50.7 us -> 50.1 us  [shards(): pl.pallas_call(functools.partial(kernel, n_seq, n_chan, halves, piece, pa...]
where the time goes in v4:
time: 52.2 us; the launch traced here: 52 us
  Pallas kernels  50.1 us (96%)
  local copies, waits for them, and re-layouts  1.88 us (4%)
    pallas_call x1, Pallas kernels, shards(): pl.pallas_call(functools.partial(kernel, n_seq, n_chan, halves, piece, pa...  50.1 us
    unnamed x1, local copies, waits for them, and re-layouts  1.88 us

profile of v4, /device:TPU:0, one launch (start us, length us, event | category | flops | bytes accessed | tf_op | source)
XLA Modules:
  0.0 52.0 jit_solution(13810379175573352513)
XLA Ops:
  0.0 50.1 %shard_map.64 = bf16[128,2048]{1,0:T(8,128)(2,1)} custom-call(bf16[128,2048]{1,0:T(8,128)(2,1)} %tokens.1, f32[3,3,1024]{2,1,0:T(4,128)} %taps.1, f32[1,1024]{1,0:T(1,128)} %bitcast.3, f32[64,2048]{1,0:T(8,128)} %filters.1, bf16[3,4096,1024]{2,1,0:T(8,128)(2,1)} %bitcast.2, bf16[1024,4096]{1,0:T(8,128)(2,1)} %w_out.1), custom_call_target="tpu_custom_call" | custom-call | tf_op jit(solution)/shard_map/pallas_call | solution.py:292
  50.1 1.9 %copy.8 = bf16[128,2048]{1,0:T(8,128)(2,1)} copy(bf16[128,2048]{1,0:T(8,128)(2,1)} %shard_map.64) | data formatting | bytes 1048576
